TPU v7x, 32 devices: a whole 2x2x4 slice. The times are simulated.
32 devices in a mesh: dp: 8 (over z, y), mp: 4 (over x, core).
Axes of the slice: x: 2, y: 2, z: 4, core: 2. Of those that a mesh axis runs over, the one named last changes fastest.
Arguments:
- tokens: bfloat16 [2048, 4096], P('dp', 'mp'), may hold values from -6 to 6
- norm_gain: float32 [4096], P('mp'), may hold values from 0.75 to 7.5
- w_gate: bfloat16 [4096, 6144], P('dp', 'mp'), may hold values from -0.09375 to 0.09375
- w_up: bfloat16 [4096, 6144], P('dp', 'mp'), may hold values from -0.09375 to 0.09375
- cotangent: bfloat16 [2048, 6144], P('dp', 'mp'), may hold values from -0.13183594 to 0.13183594
- decay_mask: int32 [2, 4096], replicated, may hold values 0 or 1
- radius: float32 [1], replicated, may hold values from 12.8 to 38.4
Outputs:
- grad_gain: float32 [4096], P('mp')
- grad_gate: float32 [4096, 6144], P('dp', 'mp')
- grad_up: float32 [4096, 6144], P('dp', 'mp')
Inputs may be any that keep to these rules, and one draw needn't show every extreme that they name: `decay_mask`: 1 marks a row that is perturbed.
All inputs are finite; a program needn't handle non-finite values.
Results may differ from a plain program's by a relative error of at most 0.024.
Values may be sent and summed in bfloat16 or wider, within the bound.
A program may use at most 128 MiB of HBM per device.

v0:
```python
import jax
import jax.numpy as jnp
from jax import lax
from jax.sharding import PartitionSpec as P


def activation(value):
    return jax.nn.gelu(value, approximate=True)


def fetch_weights(part_gate, part_up):
    return (
        lax.all_gather(part_gate, "dp", axis=0, tiled=True),
        lax.all_gather(part_up, "dp", axis=0, tiled=True),
    )


def one_pass(scaled_rows, gain_part, full_gate, full_up, cotangent):
    hidden_width = full_gate.shape[1]
    normed_part = (scaled_rows * gain_part[None, :]).astype(jnp.bfloat16)
    normed = lax.all_gather(normed_part, "mp", axis=1, tiled=True)
    pre_gate = jnp.dot(normed, full_gate, preferred_element_type=jnp.float32)
    pre_up = jnp.dot(normed, full_up, preferred_element_type=jnp.float32)
    activated, back_fn = jax.vjp(activation, pre_gate)
    upstream = cotangent.astype(jnp.float32)
    d_up = (upstream * activated).astype(jnp.bfloat16)
    d_gate = back_fn(upstream * pre_up)[0].astype(jnp.bfloat16)
    feature_term = lax.dot_general(
        d_gate, full_gate, (((1,), (1,)), ((), ())), preferred_element_type=jnp.float32
    )
    feature_term = feature_term + lax.dot_general(
        d_up, full_up, (((1,), (1,)), ((), ())), preferred_element_type=jnp.float32
    )
    d_norm = lax.psum_scatter(
        feature_term.astype(jnp.bfloat16), "mp", scatter_dimension=1, tiled=True
    ).astype(jnp.float32)
    d_gain = lax.psum(jnp.sum(d_norm * scaled_rows, axis=0), "dp")
    stacked = jnp.concatenate([d_gate, d_up], axis=1)
    both = lax.psum_scatter(
        lax.dot_general(
            normed, stacked, (((0,), (0,)), ((), ())), preferred_element_type=jnp.float32
        ).astype(jnp.bfloat16),
        "dp",
        scatter_dimension=0,
        tiled=True,
    ).astype(jnp.float32)
    return (d_gain, both[:, :hidden_width], both[:, hidden_width:])


def body(tokens, norm_gain, w_gate, w_up, cotangent, decay_mask, radius):
    values = tokens.astype(jnp.float32)
    width = values.shape[1] * lax.axis_size("mp")
    row_total = lax.psum(jnp.sum(values * values, axis=1), "mp")
    scaled_rows = values * lax.rsqrt(row_total / width + 1e-06)[:, None]
    groups = decay_mask.astype(jnp.float32)
    local_rows = w_gate.shape[0]
    first_row = lax.axis_index("dp") * local_rows
    local_groups = lax.dynamic_slice_in_dim(groups, first_row, local_rows, 1)
    gate_mask = local_groups[0][:, None]
    up_mask = local_groups[1][:, None]
    full_gate, full_up = fetch_weights(w_gate, w_up)
    asc_gain, asc_gate_f, asc_up_f = one_pass(scaled_rows, norm_gain, full_gate, full_up, cotangent)
    gate_low = asc_gate_f.astype(jnp.bfloat16)
    up_low = asc_up_f.astype(jnp.bfloat16)
    gate_wide = gate_low.astype(jnp.float32)
    up_wide = up_low.astype(jnp.float32)
    matrix_part = jnp.sum(gate_mask * gate_wide * gate_wide) + jnp.sum(up_mask * up_wide * up_wide)
    total = lax.psum(matrix_part, ("dp", "mp"))
    factor = radius[0] / (jnp.sqrt(total) + 1e-12)
    new_gate = (w_gate.astype(jnp.float32) + factor * gate_mask * gate_wide).astype(jnp.bfloat16)
    new_up = (w_up.astype(jnp.float32) + factor * up_mask * up_wide).astype(jnp.bfloat16)
    next_gate, next_up = fetch_weights(new_gate, new_up)
    return one_pass(scaled_rows, norm_gain, next_gate, next_up, cotangent)


def solution(mesh):
    placed = (P("dp", "mp"), P("mp"), P("dp", "mp"), P("dp", "mp"), P("dp", "mp"), P(), P())
    return jax.shard_map(
        body,
        mesh=mesh,
        in_specs=placed,
        out_specs=(P("mp"), P("dp", "mp"), P("dp", "mp")),
        check_vma=False,
    )
```

profile of v0, /device:TPU:0, one launch (start us, length us, event | category | flops | bytes accessed | tf_op | source)
XLA Modules:
  0.0 1715.5 jit_solution(5047203222904222491)
XLA Ops:
  7.2 1.2 fusion.33
  8.4 8.3 psum.21
  16.8 2.0 fusion.31
  18.9 0.7 all-gather.10.cloned.1.call-update
  19.6 0.7 all-gather.8.cloned.1.call-update
  20.4 21.5 %all-gather.6.cloned.1.call-done = bf16[256,4096]{1,0:T(8,128)(2,1)} async-done(((bf16[256,1024]{1,0:T(8,128)(2,1)}), bf16[256,4096]{1,0:T(8,128)(2,1)}) %all-gather.6.cloned.1.call-update) | async-done | bytes 2097168 | tf_op jit(solution)/shard_map/all_gather | solution.py:21
  41.9 178.7 %all-gather.10.cloned.1.call-done = bf16[4096,1536]{1,0:T(8,128)(2,1)} async-done(((bf16[512,1536]{1,0:T(8,128)(2,1)}), bf16[4096,1536]{1,0:T(8,128)(2,1)}) %all-gather.10.cloned.1.call-update) | async-done | bytes 12582928 | tf_op jit(solution)/shard_map/all_gather | solution.py:13
  220.6 10.1 fusion.21
  230.6 166.8 %all-gather.8.cloned.1.call-done = bf16[4096,1536]{1,0:T(8,128)(2,1)} async-done(((bf16[512,1536]{1,0:T(8,128)(2,1)}), bf16[4096,1536]{1,0:T(8,128)(2,1)}) %all-gather.8.cloned.1.call-update) | async-done | bytes 12582928 | tf_op jit(solution)/shard_map/all_gather | solution.py:14
  397.4 10.2 fusion.13
  407.6 12.8 convolution_convert_fusion.1
  420.4 0.0 all-gather.14.cloned.1.call-start
  420.5 0.7 dynamic-slice_convert_fusion
  421.2 401.4 %reduce-scatter.4.cloned.1.call-done = bf16[512,3072]{1,0:T(8,128)(2,1)} async-done(((bf16[4096,3072]{1,0:T(8,128)(2,1)}), bf16[512,3072]{1,0:T(8,128)(2,1)}) %reduce-scatter.4.cloned.1.call-update) | async-done | bytes 3145744 | tf_op jit(solution)/shard_map/reduce_scatter | solution.py:39
  822.6 4.0 fusion.6
  828.6 39.4 %psum.22 = f32[]{:T(128)} all-reduce(f32[]{:T(128)S(6)} %add.55), channel_id=1, replica_groups=mesh['dp'=8,'mp'=4] {'dp','mp'}, use_global_device_ids=true, to_apply=%region_5.0 | all-reduce | flops 1 | bytes 8 | tf_op jit(solution)/shard_map/psum | solution.py:68
  868.7 4.5 fusion.4
  873.3 0.5 all-gather.12.cloned.1.call-update
  873.8 0.2 reduce-scatter.6.cloned.1.call-start
  874.1 175.8 %all-gather.14.cloned.1.call-done = bf16[4096,1536]{1,0:T(8,128)(2,1)} async-done(((bf16[512,1536]{1,0:T(8,128)(2,1)}), bf16[4096,1536]{1,0:T(8,128)(2,1)}) %all-gather.14.cloned.1.call-update) | async-done | bytes 12582928 | tf_op jit(solution)/shard_map/all_gather | solution.py:13
  1049.8 9.5 fusion.22
  1059.3 167.8 %all-gather.12.cloned.1.call-done = bf16[4096,1536]{1,0:T(8,128)(2,1)} async-done(((bf16[512,1536]{1,0:T(8,128)(2,1)}), bf16[4096,1536]{1,0:T(8,128)(2,1)}) %all-gather.12.cloned.1.call-update) | async-done | bytes 12582928 | tf_op jit(solution)/shard_map/all_gather | solution.py:14
  1227.1 9.3 fusion.20
  1236.4 14.4 fusion.38
  1250.8 14.6 fusion
  1265.4 0.3 reduce-scatter.8.cloned.1.call-start
  1265.6 13.2 convolution_convert_fusion
  1278.9 16.2 reduce-scatter.6.cloned.1.call-done
  1295.1 1.3 fusion.32
  1296.4 22.5 %psum.23 = f32[1024]{0:T(1024)} all-reduce(f32[1024]{0:T(1024)S(1)} %fusion.32), channel_id=1, replica_groups=mesh['dp'=8,'mp'=4] {'dp'}, use_global_device_ids=true, to_apply=%region_8.0 | all-reduce | flops 1024 | bytes 8192 | tf_op jit(solution)/shard_map/psum | solution.py:37
  1318.8 384.4 %reduce-scatter.8.cloned.1.call-done = bf16[512,3072]{1,0:T(8,128)(2,1)} async-done(((bf16[4096,3072]{1,0:T(8,128)(2,1)}), bf16[512,3072]{1,0:T(8,128)(2,1)}) %reduce-scatter.8.cloned.1.call-update) | async-done | bytes 3145744 | tf_op jit(solution)/shard_map/reduce_scatter | solution.py:39
  1703.2 5.5 fusion.36
  (23 shorter events, 0.3 us)
Async XLA Ops:
  7.2 34.7 %all-gather.6.cloned.1.call-start = ((), (), s32[]{:S(2)}) async-start(), calls=%async_computation.3 | async-start | bytes 2621440 | tf_op jit(solution)/shard_map/all_gather | solution.py:21
  18.8 201.7 %all-gather.10.cloned.1.call-start = ((), (), s32[]{:S(2)}) async-start(), calls=%async_computation.5 | async-start | bytes 14155776 | tf_op jit(solution)/shard_map/all_gather | solution.py:13
  19.6 377.8 %all-gather.8.cloned.1.call-start = ((), (), s32[]{:S(2)}) async-start(), calls=%async_computation.4 | async-start | bytes 14155776 | tf_op jit(solution)/shard_map/all_gather | solution.py:14
  20.3 802.3 %reduce-scatter.4.cloned.1.call-start = ((), (), s32[]{:S(2)}) async-start(), calls=%async_computation.6 | async-start | bytes 28311552 | tf_op jit(solution)/shard_map/reduce_scatter | solution.py:39
  41.9 355.5 %copy-start.1 = (bf16[256,4096]{1,0:T(8,128)(2,1)S(1)}, bf16[256,4096]{1,0:T(8,128)(2,1)}, u32[]{:S(2)}) copy-start(bf16[256,4096]{1,0:T(8,128)(2,1)} %all-gather.6.cloned.1.call-done) | copy-start | bytes 6291460
  420.4 629.4 %all-gather.14.cloned.1.call-start = ((), (), s32[]{:S(2)}) async-start(), calls=%async_computation.8 | async-start | bytes 14155776 | tf_op jit(solution)/shard_map/all_gather | solution.py:13
  822.6 46.1 %copy-start = (bf16[512,3072]{1,0:T(8,128)(2,1)S(1)}, bf16[512,3072]{1,0:T(8,128)(2,1)}, u32[]{:S(2)}) copy-start(bf16[512,3072]{1,0:T(8,128)(2,1)} %reduce-scatter.4.cloned.1.call-done) | copy-start | bytes 9437188
  873.2 176.6 %copy-start.2 = (bf16[256,4096]{1,0:T(8,128)(2,1)S(1)}, bf16[256,4096]{1,0:T(8,128)(2,1)}, u32[]{:S(2)}) copy-start(bf16[256,4096]{1,0:T(8,128)(2,1)} %all-gather.6.cloned.1.call-done) | copy-start | bytes 6291460
  873.2 353.8 %all-gather.12.cloned.1.call-start = ((), (), s32[]{:S(2)}) async-start(), calls=%async_computation.7 | async-start | bytes 14155776 | tf_op jit(solution)/shard_map/all_gather | solution.py:14
  873.8 421.2 %reduce-scatter.6.cloned.1.call-start = ((), (), s32[]{:S(2)}) async-start(), calls=%async_computation.9 | async-start | bytes 2621440 | tf_op jit(solution)/shard_map/reduce_scatter | solution.py:34
  1236.4 14.4 copy-start.4
  1265.4 437.9 %reduce-scatter.8.cloned.1.call-start = ((), (), s32[]{:S(2)}) async-start(), calls=%async_computation.10 | async-start | bytes 28311552 | tf_op jit(solution)/shard_map/reduce_scatter | solution.py:39
  1278.9 16.2 copy-start.3
Sparse Core Ops, SparseCore 0:
  19.0 22.8 all-gather.5
  44.1 176.4 all-gather.9
  222.8 174.5 all-gather.7
  420.6 401.9 reduce-scatter.3
  873.4 176.4 all-gather.13
  1052.4 174.6 all-gather.11
  1265.5 29.5 reduce-scatter.5
  1299.4 403.7 reduce-scatter.7
where the time goes:
time: 1720 us
  waiting for transfers between devices  1510 us (88%)
  matrix products  94 us (5%)
  blocking collectives  70.2 us (4%)
    reduce_scatter x2, waiting for transfers between devices, one_pass(): lax.psum_scatter(lax.dot_general(normed, stacked, (((0,), (0,)), ((), ())...  786 us
    all_gather x2, waiting for transfers between devices, fetch_weights(): lax.all_gather(part_gate, 'dp', axis=0, tiled=True)  354 us
    all_gather x2, waiting for transfers between devices, fetch_weights(): lax.all_gather(part_up, 'dp', axis=0, tiled=True)  335 us
    psum x1, blocking collectives, body(): total = lax.psum(matrix_part, ('dp', 'mp'))  39.4 us
  transfers between devices with their start and end apart: 8, of which 8 were waited for; matrix products, arithmetic and copies ran while one was open for 2% of the time, Pallas kernels for 0%

commit v1 on v0

--- a/solution.py
+++ b/solution.py
@@ -1,7 +1,294 @@
+import functools
+
 import jax
 import jax.numpy as jnp
 from jax import lax
+from jax.experimental import pallas as pl
+from jax.experimental.pallas import tpu as pltpu
 from jax.sharding import PartitionSpec as P
+
+MESH = pl.DeviceIdType.MESH
+
+
+def remote(src, dst, send_sem, recv_sem, target):
+    return pltpu.make_async_remote_copy(
+        src_ref=src,
+        dst_ref=dst,
+        send_sem=send_sem,
+        recv_sem=recv_sem,
+        device_id=target,
+        device_id_type=MESH,
+    )
+
+
+def greet(targets):
+    barrier = pltpu.get_barrier_semaphore()
+    for target in targets:
+        pl.semaphore_signal(barrier, inc=1, device_id=target, device_id_type=MESH)
+    pl.semaphore_wait(barrier, len(targets))
+
+
+def dp_peers(n, d, q):
+    return [(lax.rem(d + k, n), q) for k in range(1, n)]
+
+
+def mp_peers(m, d, q):
+    return [(d, lax.rem(q + k, m)) for k in range(1, m)]
+
+
+def spread_kernel(
+    n, x_ref, w_ref, k_ref, xs, ws, ks, x_send, x_recv, w_send, w_recv, k_send, k_recv, own_sem
+):
+    d, q = lax.axis_index("dp"), lax.axis_index("mp")
+    rows, feats = x_ref.shape
+    depth = w_ref.shape[1]
+    zs = n // 2
+    z, y = d // 2, lax.rem(d, 2)
+    x, c = q // 2, lax.rem(q, 2)
+    other_y, other_x, other_c = (2 * z + 1 - y, q), (d, 2 * (1 - x) + c), (d, 2 * x + 1 - c)
+    greet(dp_peers(n, d, q) + [other_x, other_c])
+
+    def block(dd, qq):
+        return xs.at[
+            pl.ds(pl.multiple_of(dd * rows, rows), rows), pl.ds(pl.multiple_of(qq * feats, feats), feats)
+        ]
+
+    def w_rows(dd):
+        return ws.at[pl.ds(pl.multiple_of(dd * depth, depth), depth)]
+
+    started = []
+
+    def push(src, dd, qq, target):
+        copy = remote(src, block(dd, qq), x_send.at[len(started)], x_recv.at[dd, qq], target)
+        copy.start()
+        started.append(copy)
+
+    def arrive(dd, qq):
+        remote(block(dd, qq), block(dd, qq), x_send.at[0], x_recv.at[dd, qq], other_c).wait_recv()
+
+    own = [
+        pltpu.make_async_copy(x_ref, block(d, q), own_sem.at[0]),
+        pltpu.make_async_copy(w_ref.at[d], w_rows(d), own_sem.at[1]),
+        pltpu.make_async_copy(k_ref.at[d], ks.at[d], own_sem.at[2]),
+    ]
+    for k in range(1, zs):
+        push(x_ref, d, q, (2 * lax.rem(z + k, zs) + y, q))
+    for target in (other_y, other_x, other_c):
+        push(x_ref, d, q, target)
+    for copy in own:
+        copy.start()
+    for k in range(1, zs):
+        dd = 2 * lax.rem(z + zs - k, zs) + y
+        arrive(dd, q)
+        for target in (other_y, other_x, other_c):
+            push(block(dd, q), dd, q, target)
+    moves = []
+    for k, (dd, qq) in enumerate(dp_peers(n, d, q)):
+        moves.append(remote(w_ref.at[dd], w_rows(d), w_send.at[k], w_recv.at[d], (dd, qq)))
+        moves.append(remote(k_ref.at[dd], ks.at[d], k_send.at[k], k_recv.at[d], (dd, qq)))
+    for copy in moves:
+        copy.start()
+    for k in range(zs):
+        dd = 2 * lax.rem(z + zs - k, zs) + 1 - y
+        arrive(dd, q)
+        for target in (other_x, other_c):
+            push(block(dd, q), dd, q, target)
+    y_order = [2 * lax.rem(z + zs - k, zs) + (y if side == 0 else 1 - y) for side in (0, 1) for k in range(zs)]
+    for dd in y_order:
+        arrive(dd, other_x[1])
+        push(block(dd, other_x[1]), dd, other_x[1], other_c)
+    for qq in (other_c[1], 2 * (1 - x) + 1 - c):
+        for dd in y_order:
+            arrive(dd, qq)
+    for dd, _ in dp_peers(n, d, q):
+        remote(w_rows(dd), w_rows(dd), w_send.at[0], w_recv.at[dd], other_c).wait_recv()
+        remote(ks.at[dd], ks.at[dd], k_send.at[0], k_recv.at[dd], other_c).wait_recv()
+    for copy in started + moves:
+        copy.wait_send()
+    for copy in own:
+        copy.wait()
+
+
+def spread(n, m, x, w, k):
+    anywhere = pl.BlockSpec(memory_space=pl.ANY)
+    return pl.pallas_call(
+        functools.partial(spread_kernel, n),
+        out_shape=(
+            jax.ShapeDtypeStruct((n * x.shape[0], m * x.shape[1]), x.dtype),
+            jax.ShapeDtypeStruct((n * w.shape[1], w.shape[2]), w.dtype),
+            jax.ShapeDtypeStruct(k.shape, k.dtype),
+        ),
+        in_specs=[anywhere] * 3,
+        out_specs=(anywhere,) * 3,
+        scratch_shapes=[
+            pltpu.SemaphoreType.DMA((n * m - 1,)),
+            pltpu.SemaphoreType.DMA((n, m)),
+            pltpu.SemaphoreType.DMA((n - 1,)),
+            pltpu.SemaphoreType.DMA((n,)),
+            pltpu.SemaphoreType.DMA((n - 1,)),
+            pltpu.SemaphoreType.DMA((n,)),
+            pltpu.SemaphoreType.DMA((3,)),
+        ],
+        compiler_params=pltpu.CompilerParams(collective_id=0, has_side_effects=True),
+        name="spread",
+    )(x, w, k)
+
+
+def total_kernel(n, m, part_ref, sum_ref, dp_slots, mp_slots, dp_send, dp_recv, mp_send, mp_recv):
+    d, q = lax.axis_index("dp"), lax.axis_index("mp")
+    over_dp, over_mp = dp_peers(n, d, q), mp_peers(m, d, q)
+    greet(over_dp + over_mp)
+    sum_over(d, over_dp, part_ref, part_ref, dp_slots, dp_send, dp_recv)
+    column = functools.reduce(lambda a, b: a + b, [dp_slots[i] for i in range(n)])
+    mp_slots[q] = column
+    sends = [remote(mp_slots.at[q], mp_slots.at[q], mp_send.at[k], mp_recv.at[q], t) for k, t in enumerate(over_mp)]
+    for copy in sends:
+        copy.start()
+    for _, qq in over_mp:
+        remote(mp_slots.at[qq], mp_slots.at[qq], mp_send.at[0], mp_recv.at[qq], over_mp[0]).wait_recv()
+    for copy in sends:
+        copy.wait_send()
+    sum_ref[...] = functools.reduce(lambda a, b: a + b, [mp_slots[i] for i in range(m)])
+
+
+def sum_over(d, peers, part_ref, own_ref, slots, send, recv):
+    slots[d] = own_ref[...]
+    sends = [remote(part_ref, slots.at[d], send.at[k], recv.at[d], t) for k, t in enumerate(peers)]
+    for copy in sends:
+        copy.start()
+    for dd, _ in peers:
+        remote(slots.at[dd], slots.at[dd], send.at[0], recv.at[dd], peers[0]).wait_recv()
+    for copy in sends:
+        copy.wait_send()
+
+
+def total_sum(n, m, part):
+    return pl.pallas_call(
+        functools.partial(total_kernel, n, m),
+        out_shape=jax.ShapeDtypeStruct(part.shape, part.dtype),
+        in_specs=[pl.BlockSpec(memory_space=pltpu.VMEM)],
+        out_specs=pl.BlockSpec(memory_space=pltpu.VMEM),
+        scratch_shapes=[
+            pltpu.VMEM((n,) + part.shape, part.dtype),
+            pltpu.VMEM((m,) + part.shape, part.dtype),
+            pltpu.SemaphoreType.DMA((n - 1,)),
+            pltpu.SemaphoreType.DMA((n,)),
+            pltpu.SemaphoreType.DMA((m - 1,)),
+            pltpu.SemaphoreType.DMA((m,)),
+        ],
+        compiler_params=pltpu.CompilerParams(collective_id=1, has_side_effects=True),
+        name="total_sum",
+    )(part)
+
+
+def collect_kernel(
+    n, m, g_ref, part_ref, gs, gain_ref, dp_slots, sums, mp_slots,
+    g_send, g_recv, dp_send, dp_recv, mp_send, mp_recv, own_sem,
+):
+    d, q = lax.axis_index("dp"), lax.axis_index("mp")
+    over_dp, over_mp = dp_peers(n, d, q), mp_peers(m, d, q)
+    greet(over_dp + over_mp)
+    moves = [remote(g_ref.at[t[0]], gs.at[d], g_send.at[k], g_recv.at[d], t) for k, t in enumerate(over_dp)]
+    own = pltpu.make_async_copy(g_ref.at[d], gs.at[d], own_sem)
+    for copy in moves:
+        copy.start()
+    own.start()
+    sum_over(d, over_dp, part_ref, part_ref, dp_slots, dp_send, dp_recv)
+    sums[...] = functools.reduce(lambda a, b: a + b, [dp_slots[i] for i in range(n)])
+    mp_slots[q] = sums[q]
+    sends = [remote(sums.at[t[1]], mp_slots.at[q], mp_send.at[k], mp_recv.at[q], t) for k, t in enumerate(over_mp)]
+    for copy in sends:
+        copy.start()
+    for _, qq in over_mp:
+        remote(mp_slots.at[qq], mp_slots.at[qq], mp_send.at[0], mp_recv.at[qq], over_mp[0]).wait_recv()
+    for copy in sends:
+        copy.wait_send()
+    gain_ref[...] = functools.reduce(lambda a, b: a + b, [mp_slots[i] for i in range(m)])
+    for dd, _ in over_dp:
+        remote(gs.at[dd], gs.at[dd], g_send.at[0], g_recv.at[dd], over_dp[0]).wait_recv()
+    for copy in moves:
+        copy.wait_send()
+    own.wait()
+
+
+def collect(n, m, g, part):
+    anywhere = pl.BlockSpec(memory_space=pl.ANY)
+    inside = pl.BlockSpec(memory_space=pltpu.VMEM)
+    return pl.pallas_call(
+        functools.partial(collect_kernel, n, m),
+        out_shape=(
+            jax.ShapeDtypeStruct(g.shape, g.dtype),
+            jax.ShapeDtypeStruct(part.shape[1:], part.dtype),
+        ),
+        in_specs=[anywhere, inside],
+        out_specs=(anywhere, inside),
+        scratch_shapes=[
+            pltpu.VMEM((n,) + part.shape, part.dtype),
+            pltpu.VMEM(part.shape, part.dtype),
+            pltpu.VMEM(part.shape, part.dtype),
+            pltpu.SemaphoreType.DMA((n - 1,)),
+            pltpu.SemaphoreType.DMA((n,)),
+            pltpu.SemaphoreType.DMA((n - 1,)),
+            pltpu.SemaphoreType.DMA((n,)),
+            pltpu.SemaphoreType.DMA((m - 1,)),
+            pltpu.SemaphoreType.DMA((m,)),
+            pltpu.SemaphoreType.DMA,
+        ],
+        compiler_params=pltpu.CompilerParams(collective_id=2, has_side_effects=True),
+        name="collect",
+    )(g, part)
+
+
+def column_pass(normed, both, upstream):
+    cols = both.shape[1] // 2
+    pre = jnp.dot(normed, both, preferred_element_type=jnp.float32)
+    activated, back_fn = jax.vjp(activation, pre[:, :cols])
+    d_up = (upstream * activated).astype(jnp.bfloat16)
+    d_gate = back_fn(upstream * pre[:, cols:])[0].astype(jnp.bfloat16)
+    stacked = jnp.concatenate([d_gate, d_up], axis=1)
+    return lax.dot_general(normed, stacked, (((0,), (0,)), ((), ())), preferred_element_type=jnp.float32)
+
+
+def column_body(tokens, norm_gain, w_gate, w_up, cotangent, decay_mask, radius):
+    n, m = lax.axis_size("dp"), lax.axis_size("mp")
+    rows, feats = tokens.shape
+    depth, width = w_gate.shape
+    cols = width // n
+    values = tokens.astype(jnp.float32)
+    row_total = lax.psum(jnp.sum(values * values, axis=1), "mp")
+    scaled = values * lax.rsqrt(row_total / (feats * m) + 1e-06)[:, None]
+    normed_part = (scaled * norm_gain[None, :]).astype(jnp.bfloat16)
+
+    def by_owner(part):
+        return part.reshape(part.shape[0], n, cols).transpose(1, 0, 2)
+
+    w_blocks = jnp.concatenate([by_owner(w_gate), by_owner(w_up)], axis=2)
+    cot_blocks = by_owner(cotangent)
+    cot_blocks = jnp.concatenate([cot_blocks[:, : rows // 2], cot_blocks[:, rows // 2 :]], axis=2)
+    normed, both, cot = spread(n, m, normed_part, w_blocks, cot_blocks)
+    upstream = jnp.concatenate([cot[:, :, :cols], cot[:, :, cols:]], axis=1)
+    upstream = upstream.reshape(n * rows, cols).astype(jnp.float32)
+
+    groups = decay_mask.astype(jnp.float32)
+    is_gate = lax.broadcasted_iota(jnp.int32, (1, 2 * cols), 1) < cols
+    mask = jnp.where(is_gate, groups[0][:, None], groups[1][:, None])
+    asc = column_pass(normed, both, upstream).astype(jnp.bfloat16).astype(jnp.float32)
+    part = jnp.sum(mask * asc * asc)
+    total = total_sum(n, m, jnp.full((8, 128), part, jnp.float32))[0, 0]
+    factor = radius[0] / (jnp.sqrt(total) + 1e-12)
+    moved = (both.astype(jnp.float32) + factor * mask * asc).astype(jnp.bfloat16)
+
+    grads = column_pass(normed, moved, upstream)
+    gain_part = jnp.sum(moved.astype(jnp.float32) * grads, axis=1)
+    grads = grads.astype(jnp.bfloat16).reshape(n, depth, 2 * cols)
+    grads, gain_sum = collect(n, m, grads, gain_part.reshape(m, 8, feats // 8))
+    grads = grads.transpose(1, 0, 2).astype(jnp.float32)
+    d_gain = gain_sum.reshape(feats) / norm_gain
+    return (
+        d_gain,
+        grads[:, :, :cols].reshape(depth, width),
+        grads[:, :, cols:].reshape(depth, width),
+    )
 
 
 def activation(value):
@@ -73,10 +360,16 @@
     return one_pass(scaled_rows, norm_gain, next_gate, next_up, cotangent)
 
 
+def either_body(tokens, norm_gain, w_gate, *rest):
+    n, m = lax.axis_size("dp"), lax.axis_size("mp")
+    by_columns = m == 4 and n % 2 == 0 and (2 * w_gate.shape[1]) % (128 * n) == 0
+    return (column_body if by_columns else body)(tokens, norm_gain, w_gate, *rest)
+
+
 def solution(mesh):
     placed = (P("dp", "mp"), P("mp"), P("dp", "mp"), P("dp", "mp"), P("dp", "mp"), P(), P())
     return jax.shard_map(
-        body,
+        either_body,
         mesh=mesh,
         in_specs=placed,
         out_specs=(P("mp"), P("dp", "mp"), P("dp", "mp")),

time: 1720 us -> 355 us (0.21)
  waiting for transfers between devices: 1510 us -> 0 us
  Pallas kernels: 0 us -> 234 us
  blocking collectives: 70.2 us -> 8.34 us
  matrix products: 94 us -> 56.3 us
  local copies, waits for them, and re-layouts: 5.49 us -> 35.9 us
    reduce_scatter x3 -> x0, waiting for transfers between devices: 802 us -> none  [the longest x2 786 us: one_pass(): lax.psum_scatter(lax.dot_general(normed, stacked, (((0,), (0,)), ((), ())...]
    all_gather x5 -> x0, waiting for transfers between devices: 711 us -> none  [the longest x2 354 us: fetch_weights(): lax.all_gather(part_gate, 'dp', axis=0, tiled=True)]
    pallas_call x0 -> x3, Pallas kernels: none -> 234 us  [the longest x1 118 us: spread(): pl.pallas_call(functools.partial(spread_kernel, n), out_shape=(jax.ShapeD...]
    psum x3 -> x1, blocking collectives: 70.2 us -> 8.34 us  [column_body(): row_total = lax.psum(jnp.sum(values * values, axis=1), 'mp')]
    dot_general x8 -> x4, matrix products: 94 us -> 56.3 us  [the longest x2 32.5 us: column_pass(): lax.dot_general(normed, stacked, (((0,), (0,)), ((), ())), preferred_elem...]
  transfers between devices with their start and end apart: 8 -> 0, of which waited for: 8 -> 0; matrix products, arithmetic and copies ran while one was open for 2% -> 0% of each run, Pallas kernels for 0% -> 0%
where the time goes in v1:
time: 355 us; the launch traced here: 354 us
  Pallas kernels  234 us (66%)
  matrix products  56.3 us (16%)
  local copies, waits for them, and re-layouts  35.9 us (10%)
  other arithmetic  17.4 us (5%)
  blocking collectives  8.34 us (2%)
    pallas_call x1, Pallas kernels, spread(): pl.pallas_call(functools.partial(spread_kernel, n), out_shape=(jax.ShapeD...  118 us
    pallas_call x1, Pallas kernels, collect(): pl.pallas_call(functools.partial(collect_kernel, n, m), out_shape=(jax.Sh...  79.5 us
    pallas_call x1, Pallas kernels, total_sum(): pl.pallas_call(functools.partial(total_kernel, n, m), out_shape=jax.Shape...  36.2 us
    dot_general x2, matrix products, column_pass(): lax.dot_general(normed, stacked, (((0,), (0,)), ((), ())), preferred_elem...  32.5 us
    dot_general x2, matrix products, column_pass(): pre = jnp.dot(normed, both, preferred_element_type=jnp.float32)  23.7 us
    unnamed x15, local copies, waits for them, and re-layouts  11 us
    slice x2, local copies, waits for them, and re-layouts, column_body(): grads[:, :, cols:].reshape(depth, width)  8.38 us
    psum x1, blocking collectives, column_body(): row_total = lax.psum(jnp.sum(values * values, axis=1), 'mp')  8.34 us

profile of v1, /device:TPU:0, one launch (start us, length us, event | category | flops | bytes accessed | tf_op | source)
XLA Modules:
  0.0 354.2 jit_solution(8672600701246696366)
XLA Ops:
  1.4 1.2 fusion.24
  2.6 8.3 %psum.7 = f32[256]{0:T(256)S(1)} all-reduce(f32[256]{0:T(256)S(1)} %fusion.24), channel_id=1, replica_groups=mesh['dp'=8,'mp'=4] {'mp'}, use_global_device_ids=true, to_apply=%region_1.0 | all-reduce | flops 256 | bytes 2048 | tf_op jit(solution)/shard_map/psum | solution.py:258
  10.9 0.8 convert_element_type.56
  11.8 2.1 fusion.26.x_ref
  14.7 1.2 pad_maximum_fusion.2.k_ref
  16.1 1.6 copy.15
  17.7 2.7 copy.16
  20.4 2.6 copy.17
  23.0 3.7 %copy.18 = bf16[512,8,192]{2,0,1:T(8,128)(2,1)} copy(bf16[512,8,192]{0,2,1:T(8,128)(2,1)} %bitcast.32) | data formatting | bytes 3145728 | tf_op jit(solution)/shard_map/reshape | solution.py:263
  26.7 4.4 %pad_maximum_fusion.w_ref = bf16[8,512,384]{2,1,0:T(8,128)(2,1)} fusion(bf16[8,512,192]{2,1,0:T(8,128)(2,1)} %bitcast.30, bf16[8,512,192]{2,1,0:T(8,128)(2,1)S(1)} %bitcast.29), kind=kLoop, calls=%fused_computation.9 | loop fusion | flops 6291456 | bytes 6291456 | tf_op jit(solution)/shard_map/concatenate | solution.py:265
  31.1 118.4 %spread.1 = (bf16[2048,4096]{1,0:T(8,128)(2,1)}, bf16[4096,384]{1,0:T(8,128)(2,1)}, bf16[8,128,384]{2,1,0:T(8,128)(2,1)}) custom-call(bf16[256,1024]{1,0:T(8,128)(2,1)} %fusion.26.x_ref, bf16[8,512,384]{2,1,0:T(8,128)(2,1)} %pad_maximum_fusion.w_ref, bf16[8,128,384]{2,1,0:T(8,128)(2,1)} %pad_maximum_fusion.2.k_ref), custom_call_target="tpu_custom_call" | custom-call | tf_op jit(solution)/shard_map/spread/pallas_call | solution.py:114
  149.5 1.5 fusion.33
  151.1 1.5 bitcast_convert_fusion
  152.7 1.9 copy.24
  154.6 11.2 %fusion.35 = f32[2048,384]{0,1:T(8,128)S(1)} fusion(bf16[2048,4096]{1,0:T(8,128)(2,1)} %get-tuple-element.8, bf16[4096,384]{1,0:T(8,128)(2,1)} %get-tuple-element.10), kind=kOutput, calls=%fused_computation.57 | convolution fusion | flops 6442450944 | bytes 23068672 | tf_op jit(solution)/shard_map/dot_general | solution.py:244
  165.8 1.2 fusion.9
  167.0 15.9 %fusion.2 = (f32[]{:T(128)}, bf16[4096,384]{1,0:T(8,128)(2,1)}) fusion(f32[4096]{0:T(1024)S(1)} %bitcast.40, f32[4096]{0:T(1024)S(1)} %bitcast.37, pred[384]{0:T(512)(128)(4,1)S(1)} %iota_compare_fusion, bf16[2048,4096]{1,0:T(8,128)(2,1)} %get-tuple-element.8, bf16[2048,192]{0,1:T(8,128)(2,1)S(1)} %get-tuple-element.23, ...), kind=kOutput, calls=%fused_computation.5 | convolution fusion | flops 6455033856 | bytes 21528964 | tf_op jit(solution)/shard_map/dot_general | solution.py:249
  182.9 1.2 broadcast_in_dim.38.part_ref
  184.2 36.2 %total_sum.1 = f32[8,128]{1,0:T(8,128)} custom-call(f32[8,128]{1,0:T(8,128)} %broadcast_in_dim.38.part_ref), custom_call_target="tpu_custom_call" | custom-call | tf_op jit(solution)/shard_map/total_sum/pallas_call | solution.py:166
  220.3 1.2 slice.47
  222.2 12.5 %fusion.29 = f32[2048,384]{0,1:T(8,128)S(1)} fusion(bf16[2048,4096]{1,0:T(8,128)(2,1)} %get-tuple-element.8, bf16[4096,384]{1,0:T(8,128)(2,1)} %get-tuple-element.31, bf16[4096,384]{1,0:T(8,128)(2,1)} %get-tuple-element.10, f32[]{:T(128)S(6)} %div.14, f32[4096]{0:T(1024)S(1)} %bitcast.41, f32[4096]{0:T(1024)S(1)} %bitcast.38, ...), kind=kOutput, calls=%fused_computation.52 | convolution fusion | flops 6453460992 | bytes 26247556 | tf_op jit(solution)/shard_map/dot_general | solution.py:244
  234.8 1.2 fusion.16
  236.7 1.0 copy-done.4
  237.6 16.7 %multiply_reduce_fusion = (f32[4096]{0:T(1024)}, bf16[4096,384]{1,0:T(8,128)(2,1)}) fusion(bf16[4096,384]{1,0:T(8,128)(2,1)S(1)} %copy-done.4, f32[4096]{0:T(1024)S(1)} %bitcast.42, f32[4096]{0:T(1024)S(1)} %bitcast.39, pred[384]{0:T(512)(128)(4,1)S(1)} %iota_compare_fusion, f32[]{:T(128)S(6)} %div.14, bf16[4096,384]{1,0:T(8,128)(2,1)S(1)} %copy-done.3, ...), kind=kOutput, calls=%fused_computation.7 | convolution fusion | flops 6462894080 | bytes 27836804 | tf_op jit(solution)/shard_map/dot_general | solution.py:249
  254.3 79.5 %collect.1 = (bf16[8,512,384]{2,1,0:T(8,128)(2,1)}, f32[8,128]{1,0:T(8,128)}) custom-call(bf16[8,512,384]{2,1,0:T(8,128)(2,1)} %bitcast.35, f32[4,8,128]{2,1,0:T(8,128)} %bitcast.36), custom_call_target="tpu_custom_call" | custom-call | tf_op jit(solution)/shard_map/collect/pallas_call | solution.py:217
  333.8 1.3 bitcast_divide_fusion
  335.1 2.3 convert_bitcast_fusion
  337.4 4.6 %fusion.31 = (f32[512,8,192]{2,0,1:T(8,128)}, f32[512,8,192]{2,0,1:T(8,128)}) fusion(f32[512,8,384]{2,0,1:T(8,128)S(1)} %convert_bitcast_fusion), kind=kLoop, calls=%fused_computation.53 | loop fusion | bytes 12582912 | tf_op jit(solution)/shard_map/slice | solution.py:290
  342.0 3.7 %copy.27 = f32[512,8,192]{0,2,1:T(8,128)S(1)} copy(f32[512,8,192]{2,0,1:T(8,128)} %get-tuple-element.16) | data formatting | bytes 6291456 | tf_op jit(solution)/shard_map/slice | solution.py:290
  345.8 2.4 copy.29
  348.1 3.7 %copy.26 = f32[512,8,192]{0,2,1:T(8,128)S(1)} copy(f32[512,8,192]{2,0,1:T(8,128)} %get-tuple-element.17) | data formatting | bytes 6291456 | tf_op jit(solution)/shard_map/slice | solution.py:289
  351.9 2.4 copy.28
  (16 shorter events, 2.0 us)
Async XLA Ops:
  0.6 13.2 %copy-start.1 = (bf16[256,1536]{1,0:T(8,128)(2,1)S(1)}, bf16[256,1536]{1,0:T(8,128)(2,1)}, u32[]{:S(2)}) copy-start(bf16[256,1536]{1,0:T(8,128)(2,1)} %param.11) | copy-start | bytes 2359300
  14.6 1.5 copy-start
  234.8 1.9 copy-start.3
  234.8 2.8 copy-start.4
  254.3 79.5 %copy-start.2 = (f32[1024]{0:T(1024)S(1)}, f32[1024]{0:T(1024)}, u32[]{:S(2)}) copy-start(f32[1024]{0:T(1024)} %param.8) | copy-start | bytes 12292

commit v2 on v1

--- a/solution.py
+++ b/solution.py
@@ -8,6 +8,7 @@
 from jax.sharding import PartitionSpec as P
 
 MESH = pl.DeviceIdType.MESH
+LANES = 128
 
 
 def remote(src, dst, send_sem, recv_sem, target):
@@ -37,7 +38,7 @@
 
 
 def spread_kernel(
-    n, x_ref, w_ref, k_ref, xs, ws, ks, x_send, x_recv, w_send, w_recv, k_send, k_recv, own_sem
+    n, x_ref, w_ref, k_ref, xs, ws, ks, z_send, x_send, x_recv, w_send, w_recv, k_send, k_recv, own_sem
 ):
     d, q = lax.axis_index("dp"), lax.axis_index("mp")
     rows, feats = x_ref.shape
@@ -56,32 +57,50 @@
     def w_rows(dd):
         return ws.at[pl.ds(pl.multiple_of(dd * depth, depth), depth)]
 
-    started = []
-
-    def push(src, dd, qq, target):
-        copy = remote(src, block(dd, qq), x_send.at[len(started)], x_recv.at[dd, qq], target)
-        copy.start()
-        started.append(copy)
+    targets = (other_y, other_x, other_c)
+
+    def hop(src, kind, dd, qq):
+        return remote(src, block(dd, qq), x_send.at[kind, dd, qq], x_recv.at[dd, qq], targets[kind])
+
+    def push(src, kinds, dd, qq):
+        for kind in kinds:
+            hop(src, kind, dd, qq).start()
 
     def arrive(dd, qq):
-        remote(block(dd, qq), block(dd, qq), x_send.at[0], x_recv.at[dd, qq], other_c).wait_recv()
+        remote(block(dd, qq), block(dd, qq), x_send.at[2, dd, qq], x_recv.at[dd, qq], other_c).wait_recv()
 
     own = [
         pltpu.make_async_copy(x_ref, block(d, q), own_sem.at[0]),
         pltpu.make_async_copy(w_ref.at[d], w_rows(d), own_sem.at[1]),
         pltpu.make_async_copy(k_ref.at[d], ks.at[d], own_sem.at[2]),
     ]
+
+    def along_z(step, k):
+        origin, target = z - step * k, z + step
+        here = jnp.logical_and(origin >= 0, origin < zs)
+        onward = jnp.logical_and(here, jnp.logical_and(target >= 0, target < zs))
+        dd = 2 * lax.rem(origin + zs, zs) + y
+        target = (2 * lax.rem(target + zs, zs) + y, q)
+        src = x_ref if k == 0 else block(dd, q)
+        copy = remote(src, block(dd, q), z_send.at[(step + 1) // 2, k], x_recv.at[dd, q], target)
+        return here, onward, dd, copy
+
+    def forward(step, k):
+        here, onward, dd, copy = along_z(step, k)
+        if k > 0:
+            pl.when(here)(lambda: arrive(dd, q))
+        pl.when(onward)(lambda: copy.start())
+        if k > 0:
+            pl.when(here)(lambda: push(block(dd, q), (0, 1, 2), dd, q))
+
+    for step in (1, -1):
+        forward(step, 0)
+    push(x_ref, (0, 1, 2), d, q)
+    for copy in own:
+        copy.start()
     for k in range(1, zs):
-        push(x_ref, d, q, (2 * lax.rem(z + k, zs) + y, q))
-    for target in (other_y, other_x, other_c):
-        push(x_ref, d, q, target)
-    for copy in own:
-        copy.start()
-    for k in range(1, zs):
-        dd = 2 * lax.rem(z + zs - k, zs) + y
-        arrive(dd, q)
-        for target in (other_y, other_x, other_c):
-            push(block(dd, q), dd, q, target)
+        for step in (1, -1):
+            forward(step, k)
     moves = []
     for k, (dd, qq) in enumerate(dp_peers(n, d, q)):
         moves.append(remote(w_ref.at[dd], w_rows(d), w_send.at[k], w_recv.at[d], (dd, qq)))
@@ -91,20 +110,29 @@
     for k in range(zs):
         dd = 2 * lax.rem(z + zs - k, zs) + 1 - y
         arrive(dd, q)
-        for target in (other_x, other_c):
-            push(block(dd, q), dd, q, target)
+        push(block(dd, q), (1, 2), dd, q)
     y_order = [2 * lax.rem(z + zs - k, zs) + (y if side == 0 else 1 - y) for side in (0, 1) for k in range(zs)]
     for dd in y_order:
         arrive(dd, other_x[1])
-        push(block(dd, other_x[1]), dd, other_x[1], other_c)
+        push(block(dd, other_x[1]), (2,), dd, other_x[1])
     for qq in (other_c[1], 2 * (1 - x) + 1 - c):
         for dd in y_order:
             arrive(dd, qq)
     for dd, _ in dp_peers(n, d, q):
         remote(w_rows(dd), w_rows(dd), w_send.at[0], w_recv.at[dd], other_c).wait_recv()
         remote(ks.at[dd], ks.at[dd], k_send.at[0], k_recv.at[dd], other_c).wait_recv()
-    for copy in started + moves:
+    for copy in moves:
         copy.wait_send()
+    for dd in y_order:
+        hop(block(dd, q), 1, dd, q).wait_send()
+        for qq in (q, other_x[1]):
+            hop(block(dd, qq), 2, dd, qq).wait_send()
+    for dd in y_order[:zs]:
+        hop(block(dd, q), 0, dd, q).wait_send()
+    for k in range(zs):
+        for step in (1, -1):
+            _, onward, _, copy = along_z(step, k)
+            pl.when(onward)(lambda copy=copy: copy.wait_send())
     for copy in own:
         copy.wait()
 
@@ -121,7 +149,8 @@
         in_specs=[anywhere] * 3,
         out_specs=(anywhere,) * 3,
         scratch_shapes=[
-            pltpu.SemaphoreType.DMA((n * m - 1,)),
+            pltpu.SemaphoreType.DMA((2, n // 2)),
+            pltpu.SemaphoreType.DMA((3, n, m)),
             pltpu.SemaphoreType.DMA((n, m)),
             pltpu.SemaphoreType.DMA((n - 1,)),
             pltpu.SemaphoreType.DMA((n,)),
@@ -239,13 +268,79 @@
     )(g, part)
 
 
+def swap_halves(tile):
+    return pltpu.roll(tile, LANES // 2, 1)
+
+
+def by_owner_kernel(a_ref, b_ref, out_ref):
+    left = lax.broadcasted_iota(jnp.int32, (a_ref.shape[0], LANES), 1) < LANES // 2
+    for p in range(out_ref.shape[0] // 2):
+        first, middle, last = (pl.ds((3 * p + i) * LANES, LANES) for i in range(3))
+        a_mid = a_ref[:, middle].astype(jnp.float32)
+        b_mid = b_ref[:, middle].astype(jnp.float32)
+        out_ref[2 * p, :, :LANES] = a_ref[:, first]
+        out_ref[2 * p, :, LANES : 2 * LANES] = jnp.where(left, a_mid, swap_halves(b_mid)).astype(out_ref.dtype)
+        out_ref[2 * p, :, 2 * LANES :] = b_ref[:, first]
+        out_ref[2 * p + 1, :, :LANES] = a_ref[:, last]
+        out_ref[2 * p + 1, :, LANES : 2 * LANES] = jnp.where(left, swap_halves(a_mid), b_mid).astype(out_ref.dtype)
+        out_ref[2 * p + 1, :, 2 * LANES :] = b_ref[:, last]
+
+
+def by_owner(n, a, b, rows, b_from=0):
+    step = min(rows, 128)
+    width = a.shape[1]
+    return pl.pallas_call(
+        by_owner_kernel,
+        grid=(rows // step,),
+        out_shape=jax.ShapeDtypeStruct((n, rows, 3 * LANES), a.dtype),
+        in_specs=[
+            pl.BlockSpec((step, width), lambda i: (i, 0)),
+            pl.BlockSpec((step, width), lambda i: (i + b_from // step, 0)),
+        ],
+        out_specs=pl.BlockSpec((n, step, 3 * LANES), lambda i: (0, i, 0)),
+        compiler_params=pltpu.CompilerParams(vmem_limit_bytes=24 * 2**20),
+        name="by_owner",
+    )(a, b)
+
+
+def in_place_kernel(g_ref, gate_ref, up_ref):
+    left = lax.broadcasted_iota(jnp.int32, (g_ref.shape[1], LANES), 1) < LANES // 2
+    for p in range(g_ref.shape[0] // 2):
+        first, middle, last = (pl.ds((3 * p + i) * LANES, LANES) for i in range(3))
+        one = g_ref[2 * p].astype(jnp.float32)
+        two = g_ref[2 * p + 1].astype(jnp.float32)
+        one_mid, two_mid = one[:, LANES : 2 * LANES], two[:, LANES : 2 * LANES]
+        gate_ref[:, first] = one[:, :LANES]
+        gate_ref[:, middle] = jnp.where(left, one_mid, swap_halves(two_mid))
+        gate_ref[:, last] = two[:, :LANES]
+        up_ref[:, first] = one[:, 2 * LANES :]
+        up_ref[:, middle] = jnp.where(left, swap_halves(one_mid), two_mid)
+        up_ref[:, last] = two[:, 2 * LANES :]
+
+
+def in_place(g, width):
+    n, rows, share = g.shape
+    step = 64
+    whole = pl.BlockSpec((step, width), lambda i: (i, 0))
+    return pl.pallas_call(
+        in_place_kernel,
+        grid=(rows // step,),
+        out_shape=(jax.ShapeDtypeStruct((rows, width), jnp.float32),) * 2,
+        in_specs=[pl.BlockSpec((n, step, share), lambda i: (0, i, 0))],
+        out_specs=(whole, whole),
+        compiler_params=pltpu.CompilerParams(vmem_limit_bytes=24 * 2**20),
+        name="in_place",
+    )(g)
+
+
 def column_pass(normed, both, upstream):
     cols = both.shape[1] // 2
     pre = jnp.dot(normed, both, preferred_element_type=jnp.float32)
+    pre_up = jnp.concatenate([pre[:, 2 * LANES :], pre[:, cols : 2 * LANES]], axis=1)
     activated, back_fn = jax.vjp(activation, pre[:, :cols])
     d_up = (upstream * activated).astype(jnp.bfloat16)
-    d_gate = back_fn(upstream * pre[:, cols:])[0].astype(jnp.bfloat16)
-    stacked = jnp.concatenate([d_gate, d_up], axis=1)
+    d_gate = back_fn(upstream * pre_up)[0].astype(jnp.bfloat16)
+    stacked = jnp.concatenate([d_gate, d_up[:, LANES:], d_up[:, :LANES]], axis=1)
     return lax.dot_general(normed, stacked, (((0,), (0,)), ((), ())), preferred_element_type=jnp.float32)
 
 
@@ -259,14 +354,12 @@
     scaled = values * lax.rsqrt(row_total / (feats * m) + 1e-06)[:, None]
     normed_part = (scaled * norm_gain[None, :]).astype(jnp.bfloat16)
 
-    def by_owner(part):
-        return part.reshape(part.shape[0], n, cols).transpose(1, 0, 2)
-
-    w_blocks = jnp.concatenate([by_owner(w_gate), by_owner(w_up)], axis=2)
-    cot_blocks = by_owner(cotangent)
-    cot_blocks = jnp.concatenate([cot_blocks[:, : rows // 2], cot_blocks[:, rows // 2 :]], axis=2)
+    w_blocks = by_owner(n, w_gate, w_up, depth)
+    cot_blocks = by_owner(n, cotangent, cotangent, rows // 2, rows // 2)
     normed, both, cot = spread(n, m, normed_part, w_blocks, cot_blocks)
-    upstream = jnp.concatenate([cot[:, :, :cols], cot[:, :, cols:]], axis=1)
+    whole_tile = jnp.concatenate([cot[:, :, :LANES], cot[:, :, 2 * LANES :]], axis=1)
+    half_tile = jnp.concatenate([cot[:, :, LANES:cols], cot[:, :, cols : 2 * LANES]], axis=1)
+    upstream = jnp.concatenate([whole_tile, half_tile], axis=2)
     upstream = upstream.reshape(n * rows, cols).astype(jnp.float32)
 
     groups = decay_mask.astype(jnp.float32)
@@ -282,13 +375,8 @@
     gain_part = jnp.sum(moved.astype(jnp.float32) * grads, axis=1)
     grads = grads.astype(jnp.bfloat16).reshape(n, depth, 2 * cols)
     grads, gain_sum = collect(n, m, grads, gain_part.reshape(m, 8, feats // 8))
-    grads = grads.transpose(1, 0, 2).astype(jnp.float32)
     d_gain = gain_sum.reshape(feats) / norm_gain
-    return (
-        d_gain,
-        grads[:, :, :cols].reshape(depth, width),
-        grads[:, :, cols:].reshape(depth, width),
-    )
+    return (d_gain,) + tuple(in_place(grads, width))
 
 
 def activation(value):
@@ -362,7 +450,7 @@
 
 def either_body(tokens, norm_gain, w_gate, *rest):
     n, m = lax.axis_size("dp"), lax.axis_size("mp")
-    by_columns = m == 4 and n % 2 == 0 and (2 * w_gate.shape[1]) % (128 * n) == 0
+    by_columns = m == 4 and n % 2 == 0 and 2 * w_gate.shape[1] == 3 * LANES * n
     return (column_body if by_columns else body)(tokens, norm_gain, w_gate, *rest)
 
 

time: 355 us -> 325 us (0.915)
  local copies, waits for them, and re-layouts: 35.9 us -> 12.9 us
  other arithmetic: 17.4 us -> 9.68 us
    pallas_call x1, Pallas kernels: 36.2 us -> 13.6 us  [total_sum(): pl.pallas_call(functools.partial(total_kernel, n, m), out_shape=jax.Shape...]
    pallas_call x1, Pallas kernels: 118 us -> 137 us  [spread(): pl.pallas_call(functools.partial(spread_kernel, n), out_shape=(jax.ShapeD...]
    slice x5 -> x10, local copies, waits for them, and re-layouts: 13.7 us -> 2.6 us  [the longest x1 1.17 us: column_body(): cot[:, :, LANES:cols]]
    reshape x3 -> x0, local copies, waits for them, and re-layouts: 6.94 us -> none  [by_owner(): return part.reshape(part.shape[0], n, cols).transpose(1, 0, 2)]
    pallas_call x0 -> x3, Pallas kernels: none -> 5.64 us  [the longest x1 4.36 us: in_place(): pl.pallas_call(in_place_kernel, grid=(rows // step,), out_shape=(jax.Shap...]
    concatenate x3 -> x1, other arithmetic: 5.76 us -> 0.22 us  [column_body(): upstream = jnp.concatenate([whole_tile, half_tile], axis=2)]
    unnamed x15 -> x18, local copies, waits for them, and re-layouts: 11 us -> 5.95 us
where the time goes in v2:
time: 325 us
  Pallas kernels  235 us (72%)
  matrix products  56.3 us (17%)
  local copies, waits for them, and re-layouts  12.9 us (4%)
  other arithmetic  9.68 us (3%)
  blocking collectives  8.34 us (3%)
    pallas_call x1, Pallas kernels, spread(): pl.pallas_call(functools.partial(spread_kernel, n), out_shape=(jax.ShapeD...  137 us
    pallas_call x1, Pallas kernels, collect(): pl.pallas_call(functools.partial(collect_kernel, n, m), out_shape=(jax.Sh...  79.5 us
    dot_general x2, matrix products, column_pass(): lax.dot_general(normed, stacked, (((0,), (0,)), ((), ())), preferred_elem...  32.5 us
    dot_general x2, matrix products, column_pass(): pre = jnp.dot(normed, both, preferred_element_type=jnp.float32)  23.7 us
    pallas_call x1, Pallas kernels, total_sum(): pl.pallas_call(functools.partial(total_kernel, n, m), out_shape=jax.Shape...  13.6 us
    psum x1, blocking collectives, column_body(): row_total = lax.psum(jnp.sum(values * values, axis=1), 'mp')  8.34 us

profile of v2, /device:TPU:0, one launch (start us, length us, event | category | flops | bytes accessed | tf_op | source)
XLA Modules:
  0.0 324.8 jit_solution(6757393572586589418)
XLA Ops:
  1.5 1.2 fusion.28
  2.7 8.3 %psum.7 = f32[256]{0:T(256)S(1)} all-reduce(f32[256]{0:T(256)S(1)} %fusion.28), channel_id=1, replica_groups=mesh['dp'=8,'mp'=4] {'mp'}, use_global_device_ids=true, to_apply=%region_1.0 | all-reduce | flops 256 | bytes 2048 | tf_op jit(solution)/shard_map/psum | solution.py:353
  11.0 0.9 convert_element_type.50
  12.0 2.0 fusion.30.x_ref
  14.0 0.2 by_owner.3.k_ref
  14.2 0.0 copy-start.3
  14.2 0.9 copy-done.3
  15.1 1.1 by_owner.2.w_ref
  16.2 1.7 copy-done
  17.8 136.5 %spread.1 = (bf16[2048,4096]{1,0:T(8,128)(2,1)}, bf16[4096,384]{1,0:T(8,128)(2,1)}, bf16[8,128,384]{2,1,0:T(8,128)(2,1)}) custom-call(bf16[256,1024]{1,0:T(8,128)(2,1)} %fusion.30.x_ref, bf16[8,512,384]{2,1,0:T(8,128)(2,1)} %copy-done, bf16[8,128,384]{2,1,0:T(8,128)(2,1)} %copy-done.3), custom_call_target="tpu_custom_call" | custom-call | tf_op jit(solution)/shard_map/spread/pallas_call | solution.py:142
  154.4 1.2 fusion.36
  155.6 1.1 fusion.35
  156.6 0.2 maximum_maximum_fusion
  156.9 1.5 bitcast_convert_fusion
  158.4 1.9 copy.13
  160.3 11.2 %fusion.38 = f32[2048,384]{0,1:T(8,128)S(1)} fusion(bf16[2048,4096]{1,0:T(8,128)(2,1)} %get-tuple-element.10, bf16[4096,384]{1,0:T(8,128)(2,1)} %get-tuple-element.12), kind=kOutput, calls=%fused_computation.57 | convolution fusion | flops 6442450944 | bytes 23068672 | tf_op jit(solution)/shard_map/dot_general | solution.py:338
  171.6 0.1 slice.70
  171.7 1.2 fusion.9
  173.0 15.9 %fusion.2 = (f32[]{:T(128)}, bf16[4096,384]{1,0:T(8,128)(2,1)}) fusion(f32[4096]{0:T(1024)S(1)} %bitcast.22, f32[4096]{0:T(1024)S(1)} %bitcast.19, pred[384]{0:T(512)(128)(4,1)S(1)} %iota_compare_fusion, bf16[2048,4096]{1,0:T(8,128)(2,1)} %get-tuple-element.10, bf16[2048,128]{0,1:T(8,128)(2,1)S(1)} %slice.74, bf16[2048,64]{0,1:T(8,128)(2,1)S(1)} %slice.73, ...), kind=kOutput, calls=%fused_computation.5 | convolution fusion | flops 6456606720 | bytes 21528964 | tf_op jit(solution)/shard_map/dot_general | solution.py:344
  188.9 1.2 broadcast_in_dim.38.part_ref
  190.1 13.6 %total_sum.1 = f32[8,128]{1,0:T(8,128)} custom-call(f32[8,128]{1,0:T(8,128)} %broadcast_in_dim.38.part_ref), custom_call_target="tpu_custom_call" | custom-call | tf_op jit(solution)/shard_map/total_sum/pallas_call | solution.py:195
  203.7 1.2 slice.62
  205.6 12.5 %fusion.33 = f32[2048,384]{0,1:T(8,128)S(1)} fusion(bf16[2048,4096]{1,0:T(8,128)(2,1)} %get-tuple-element.10, bf16[4096,384]{1,0:T(8,128)(2,1)} %get-tuple-element.30, bf16[4096,384]{1,0:T(8,128)(2,1)} %get-tuple-element.12, f32[]{:T(128)S(6)} %div.14, f32[4096]{0:T(1024)S(1)} %bitcast.23, f32[4096]{0:T(1024)S(1)} %bitcast.20, ...), kind=kOutput, calls=%fused_computation.53 | convolution fusion | flops 6453460992 | bytes 26247556 | tf_op jit(solution)/shard_map/dot_general | solution.py:338
  218.2 0.1 slice.75
  218.3 1.2 fusion.16
  219.6 0.5 copy-done.7
  220.2 1.0 copy-done.8
  221.1 16.7 %multiply_reduce_fusion = (f32[4096]{0:T(1024)}, bf16[4096,384]{1,0:T(8,128)(2,1)}) fusion(bf16[4096,384]{1,0:T(8,128)(2,1)S(1)} %copy-done.8, f32[4096]{0:T(1024)S(1)} %bitcast.24, f32[4096]{0:T(1024)S(1)} %bitcast.21, pred[384]{0:T(512)(128)(4,1)S(1)} %iota_compare_fusion, f32[]{:T(128)S(6)} %div.14, bf16[4096,384]{1,0:T(8,128)(2,1)S(1)} %copy-done.7, ...), kind=kOutput, calls=%fused_computation.6 | convolution fusion | flops 6464466944 | bytes 27836804 | tf_op jit(solution)/shard_map/dot_general | solution.py:344
  237.8 79.5 %collect.1 = (bf16[8,512,384]{2,1,0:T(8,128)(2,1)}, f32[8,128]{1,0:T(8,128)}) custom-call(bf16[8,512,384]{2,1,0:T(8,128)(2,1)} %bitcast.17, f32[4,8,128]{2,1,0:T(8,128)} %bitcast.18), custom_call_target="tpu_custom_call" | custom-call | tf_op jit(solution)/shard_map/collect/pallas_call | solution.py:246
  317.3 1.3 bitcast_divide_fusion
  318.5 1.9 copy-done.1
  320.4 4.4 %in_place.1 = (f32[512,1536]{1,0:T(8,128)}, f32[512,1536]{1,0:T(8,128)}) custom-call(bf16[8,512,384]{2,1,0:T(8,128)(2,1)S(1)} %copy-done.1), custom_call_target="tpu_custom_call" | custom-call | tf_op jit(solution)/shard_map/in_place/pallas_call | solution.py:325
  (21 shorter events, 0.3 us)
Async XLA Ops:
  0.6 13.4 %copy-start.2 = (bf16[256,1536]{1,0:T(8,128)(2,1)S(1)}, bf16[256,1536]{1,0:T(8,128)(2,1)}, u32[]{:S(2)}) copy-start(bf16[256,1536]{1,0:T(8,128)(2,1)} %b_ref.3) | copy-start | bytes 2359300
  0.6 14.4 %copy-start.4 = (bf16[512,1536]{1,0:T(8,128)(2,1)S(1)}, bf16[512,1536]{1,0:T(8,128)(2,1)}, u32[]{:S(2)}) copy-start(bf16[512,1536]{1,0:T(8,128)(2,1)} %a_ref.2) | copy-start | bytes 4718596
  11.0 4.0 %copy-start.5 = (bf16[512,1536]{1,0:T(8,128)(2,1)S(1)}, bf16[512,1536]{1,0:T(8,128)(2,1)}, u32[]{:S(2)}) copy-start(bf16[512,1536]{1,0:T(8,128)(2,1)} %b_ref.2) | copy-start | bytes 4718596
  14.2 0.9 copy-start.3
  16.2 1.7 copy-start
  218.3 1.9 copy-start.7
  218.3 2.8 copy-start.8
  237.8 79.5 %copy-start.6 = (f32[1024]{0:T(1024)S(1)}, f32[1024]{0:T(1024)}, u32[]{:S(2)}) copy-start(f32[1024]{0:T(1024)} %param.8) | copy-start | bytes 12292
  318.5 1.9 copy-start.1

commit v3 on v2

--- a/solution.py
+++ b/solution.py
@@ -98,15 +98,16 @@
     push(x_ref, (0, 1, 2), d, q)
     for copy in own:
         copy.start()
-    for k in range(1, zs):
-        for step in (1, -1):
-            forward(step, k)
     moves = []
     for k, (dd, qq) in enumerate(dp_peers(n, d, q)):
         moves.append(remote(w_ref.at[dd], w_rows(d), w_send.at[k], w_recv.at[d], (dd, qq)))
         moves.append(remote(k_ref.at[dd], ks.at[d], k_send.at[k], k_recv.at[d], (dd, qq)))
-    for copy in moves:
-        copy.start()
+    for k in range(1, zs):
+        for step in (1, -1):
+            forward(step, k)
+        if k == 1:
+            for copy in moves:
+                copy.start()
     for k in range(zs):
         dd = 2 * lax.rem(z + zs - k, zs) + 1 - y
         arrive(dd, q)

time: 325 us -> 350 us (1.077)
  Pallas kernels: 235 us -> 260 us
    pallas_call x1, Pallas kernels: 137 us -> 165 us  [spread(): pl.pallas_call(functools.partial(spread_kernel, n), out_shape=(jax.ShapeD...]
    pallas_call x1, Pallas kernels: 13.6 us -> 9.19 us  [total_sum(): pl.pallas_call(functools.partial(total_kernel, n, m), out_shape=jax.Shape...]
where the time goes in v3:
time: 350 us
  Pallas kernels  260 us (74%)
  matrix products  56.3 us (16%)
  local copies, waits for them, and re-layouts  12.9 us (4%)
  other arithmetic  9.68 us (3%)
  blocking collectives  8.34 us (2%)
    pallas_call x1, Pallas kernels, spread(): pl.pallas_call(functools.partial(spread_kernel, n), out_shape=(jax.ShapeD...  165 us
    pallas_call x1, Pallas kernels, collect(): pl.pallas_call(functools.partial(collect_kernel, n, m), out_shape=(jax.Sh...  80 us
    dot_general x2, matrix products, column_pass(): lax.dot_general(normed, stacked, (((0,), (0,)), ((), ())), preferred_elem...  32.5 us
    dot_general x2, matrix products, column_pass(): pre = jnp.dot(normed, both, preferred_element_type=jnp.float32)  23.7 us
    pallas_call x1, Pallas kernels, total_sum(): pl.pallas_call(functools.partial(total_kernel, n, m), out_shape=jax.Shape...  9.19 us
    psum x1, blocking collectives, column_body(): row_total = lax.psum(jnp.sum(values * values, axis=1), 'mp')  8.34 us

profile of v3, /device:TPU:0, one launch (start us, length us, event | category | flops | bytes accessed | tf_op | source)
XLA Modules:
  0.0 349.8 jit_solution(16393732051512587130)
XLA Ops:
  1.5 1.2 fusion.28
  2.7 8.3 %psum.7 = f32[256]{0:T(256)S(1)} all-reduce(f32[256]{0:T(256)S(1)} %fusion.28), channel_id=1, replica_groups=mesh['dp'=8,'mp'=4] {'mp'}, use_global_device_ids=true, to_apply=%region_1.0 | all-reduce | flops 256 | bytes 2048 | tf_op jit(solution)/shard_map/psum | solution.py:354
  11.0 0.9 convert_element_type.50
  12.0 2.0 fusion.30.x_ref
  14.0 0.2 by_owner.3.k_ref
  14.2 0.0 copy-start.3
  14.2 0.9 copy-done.3
  15.1 1.1 by_owner.2.w_ref
  16.2 1.7 copy-done
  17.8 165.3 %spread.1 = (bf16[2048,4096]{1,0:T(8,128)(2,1)}, bf16[4096,384]{1,0:T(8,128)(2,1)}, bf16[8,128,384]{2,1,0:T(8,128)(2,1)}) custom-call(bf16[256,1024]{1,0:T(8,128)(2,1)} %fusion.30.x_ref, bf16[8,512,384]{2,1,0:T(8,128)(2,1)} %copy-done, bf16[8,128,384]{2,1,0:T(8,128)(2,1)} %copy-done.3), custom_call_target="tpu_custom_call" | custom-call | tf_op jit(solution)/shard_map/spread/pallas_call | solution.py:143
  183.2 1.2 fusion.36
  184.4 1.1 fusion.35
  185.4 0.2 maximum_maximum_fusion
  185.7 1.5 bitcast_convert_fusion
  187.2 1.9 copy.13
  189.1 11.2 %fusion.38 = f32[2048,384]{0,1:T(8,128)S(1)} fusion(bf16[2048,4096]{1,0:T(8,128)(2,1)} %get-tuple-element.10, bf16[4096,384]{1,0:T(8,128)(2,1)} %get-tuple-element.12), kind=kOutput, calls=%fused_computation.57 | convolution fusion | flops 6442450944 | bytes 23068672 | tf_op jit(solution)/shard_map/dot_general | solution.py:339
  200.4 0.1 slice.70
  200.5 1.2 fusion.9
  201.8 15.9 %fusion.2 = (f32[]{:T(128)}, bf16[4096,384]{1,0:T(8,128)(2,1)}) fusion(f32[4096]{0:T(1024)S(1)} %bitcast.22, f32[4096]{0:T(1024)S(1)} %bitcast.19, pred[384]{0:T(512)(128)(4,1)S(1)} %iota_compare_fusion, bf16[2048,4096]{1,0:T(8,128)(2,1)} %get-tuple-element.10, bf16[2048,128]{0,1:T(8,128)(2,1)S(1)} %slice.74, bf16[2048,64]{0,1:T(8,128)(2,1)S(1)} %slice.73, ...), kind=kOutput, calls=%fused_computation.5 | convolution fusion | flops 6456606720 | bytes 21528964 | tf_op jit(solution)/shard_map/dot_general | solution.py:345
  217.7 1.2 broadcast_in_dim.38.part_ref
  218.9 9.2 %total_sum.1 = f32[8,128]{1,0:T(8,128)} custom-call(f32[8,128]{1,0:T(8,128)} %broadcast_in_dim.38.part_ref), custom_call_target="tpu_custom_call" | custom-call | tf_op jit(solution)/shard_map/total_sum/pallas_call | solution.py:196
  228.1 1.2 slice.62
  230.0 12.5 %fusion.33 = f32[2048,384]{0,1:T(8,128)S(1)} fusion(bf16[2048,4096]{1,0:T(8,128)(2,1)} %get-tuple-element.10, bf16[4096,384]{1,0:T(8,128)(2,1)} %get-tuple-element.30, bf16[4096,384]{1,0:T(8,128)(2,1)} %get-tuple-element.12, f32[]{:T(128)S(6)} %div.14, f32[4096]{0:T(1024)S(1)} %bitcast.23, f32[4096]{0:T(1024)S(1)} %bitcast.20, ...), kind=kOutput, calls=%fused_computation.53 | convolution fusion | flops 6453460992 | bytes 26247556 | tf_op jit(solution)/shard_map/dot_general | solution.py:339
  242.6 0.1 slice.75
  242.7 1.2 fusion.16
  244.0 0.5 copy-done.7
  244.6 1.0 copy-done.8
  245.5 16.7 %multiply_reduce_fusion = (f32[4096]{0:T(1024)}, bf16[4096,384]{1,0:T(8,128)(2,1)}) fusion(bf16[4096,384]{1,0:T(8,128)(2,1)S(1)} %copy-done.8, f32[4096]{0:T(1024)S(1)} %bitcast.24, f32[4096]{0:T(1024)S(1)} %bitcast.21, pred[384]{0:T(512)(128)(4,1)S(1)} %iota_compare_fusion, f32[]{:T(128)S(6)} %div.14, bf16[4096,384]{1,0:T(8,128)(2,1)S(1)} %copy-done.7, ...), kind=kOutput, calls=%fused_computation.6 | convolution fusion | flops 6464466944 | bytes 27836804 | tf_op jit(solution)/shard_map/dot_general | solution.py:345
  262.2 80.0 %collect.1 = (bf16[8,512,384]{2,1,0:T(8,128)(2,1)}, f32[8,128]{1,0:T(8,128)}) custom-call(bf16[8,512,384]{2,1,0:T(8,128)(2,1)} %bitcast.17, f32[4,8,128]{2,1,0:T(8,128)} %bitcast.18), custom_call_target="tpu_custom_call" | custom-call | tf_op jit(solution)/shard_map/collect/pallas_call | solution.py:247
  342.3 1.3 bitcast_divide_fusion
  343.5 1.9 copy-done.1
  345.4 4.4 %in_place.1 = (f32[512,1536]{1,0:T(8,128)}, f32[512,1536]{1,0:T(8,128)}) custom-call(bf16[8,512,384]{2,1,0:T(8,128)(2,1)S(1)} %copy-done.1), custom_call_target="tpu_custom_call" | custom-call | tf_op jit(solution)/shard_map/in_place/pallas_call | solution.py:326
  (21 shorter events, 0.3 us)
Async XLA Ops:
  0.6 13.4 %copy-start.2 = (bf16[256,1536]{1,0:T(8,128)(2,1)S(1)}, bf16[256,1536]{1,0:T(8,128)(2,1)}, u32[]{:S(2)}) copy-start(bf16[256,1536]{1,0:T(8,128)(2,1)} %b_ref.3) | copy-start | bytes 2359300
  0.6 14.4 %copy-start.4 = (bf16[512,1536]{1,0:T(8,128)(2,1)S(1)}, bf16[512,1536]{1,0:T(8,128)(2,1)}, u32[]{:S(2)}) copy-start(bf16[512,1536]{1,0:T(8,128)(2,1)} %a_ref.2) | copy-start | bytes 4718596
  11.0 4.0 %copy-start.5 = (bf16[512,1536]{1,0:T(8,128)(2,1)S(1)}, bf16[512,1536]{1,0:T(8,128)(2,1)}, u32[]{:S(2)}) copy-start(bf16[512,1536]{1,0:T(8,128)(2,1)} %b_ref.2) | copy-start | bytes 4718596
  14.2 0.9 copy-start.3
  16.2 1.7 copy-start
  242.7 1.9 copy-start.7
  242.7 2.8 copy-start.8
  262.2 80.0 %copy-start.6 = (f32[1024]{0:T(1024)S(1)}, f32[1024]{0:T(1024)}, u32[]{:S(2)}) copy-start(f32[1024]{0:T(1024)} %param.8) | copy-start | bytes 12292
  343.5 1.9 copy-start.1

commit v4 on v3

--- a/solution.py
+++ b/solution.py
@@ -105,7 +105,7 @@
     for k in range(1, zs):
         for step in (1, -1):
             forward(step, k)
-        if k == 1:
+        if k == zs - 2:
             for copy in moves:
                 copy.start()
     for k in range(zs):

time: 350 us -> 344 us (0.983)
  Pallas kernels: 260 us -> 253 us
    pallas_call x1, Pallas kernels: 165 us -> 155 us  [spread(): pl.pallas_call(functools.partial(spread_kernel, n), out_shape=(jax.ShapeD...]
    pallas_call x1, Pallas kernels: 9.19 us -> 14.9 us  [total_sum(): pl.pallas_call(functools.partial(total_kernel, n, m), out_shape=jax.Shape...]
where the time goes in v4:
time: 344 us; the launch traced here: 343 us
  Pallas kernels  253 us (74%)
  matrix products  56.3 us (16%)
  local copies, waits for them, and re-layouts  12.9 us (4%)
  other arithmetic  9.68 us (3%)
  blocking collectives  8.34 us (2%)
    pallas_call x1, Pallas kernels, spread(): pl.pallas_call(functools.partial(spread_kernel, n), out_shape=(jax.ShapeD...  155 us
    pallas_call x1, Pallas kernels, collect(): pl.pallas_call(functools.partial(collect_kernel, n, m), out_shape=(jax.Sh...  77.8 us
    dot_general x2, matrix products, column_pass(): lax.dot_general(normed, stacked, (((0,), (0,)), ((), ())), preferred_elem...  32.5 us
    dot_general x2, matrix products, column_pass(): pre = jnp.dot(normed, both, preferred_element_type=jnp.float32)  23.7 us
    pallas_call x1, Pallas kernels, total_sum(): pl.pallas_call(functools.partial(total_kernel, n, m), out_shape=jax.Shape...  14.9 us
    psum x1, blocking collectives, column_body(): row_total = lax.psum(jnp.sum(values * values, axis=1), 'mp')  8.34 us

profile of v4, /device:TPU:0, one launch (start us, length us, event | category | flops | bytes accessed | tf_op | source)
XLA Modules:
  0.0 343.0 jit_solution(17227452591367093844)
XLA Ops:
  1.5 1.2 fusion.28
  2.7 8.3 %psum.7 = f32[256]{0:T(256)S(1)} all-reduce(f32[256]{0:T(256)S(1)} %fusion.28), channel_id=1, replica_groups=mesh['dp'=8,'mp'=4] {'mp'}, use_global_device_ids=true, to_apply=%region_1.0 | all-reduce | flops 256 | bytes 2048 | tf_op jit(solution)/shard_map/psum | solution.py:354
  11.0 0.9 convert_element_type.50
  12.0 2.0 fusion.30.x_ref
  14.0 0.2 by_owner.3.k_ref
  14.2 0.0 copy-start.3
  14.2 0.9 copy-done.3
  15.1 1.1 by_owner.2.w_ref
  16.2 1.7 copy-done
  17.8 155.1 %spread.1 = (bf16[2048,4096]{1,0:T(8,128)(2,1)}, bf16[4096,384]{1,0:T(8,128)(2,1)}, bf16[8,128,384]{2,1,0:T(8,128)(2,1)}) custom-call(bf16[256,1024]{1,0:T(8,128)(2,1)} %fusion.30.x_ref, bf16[8,512,384]{2,1,0:T(8,128)(2,1)} %copy-done, bf16[8,128,384]{2,1,0:T(8,128)(2,1)} %copy-done.3), custom_call_target="tpu_custom_call" | custom-call | tf_op jit(solution)/shard_map/spread/pallas_call | solution.py:143
  173.0 1.2 fusion.36
  174.1 1.1 fusion.35
  175.2 0.2 maximum_maximum_fusion
  175.4 1.5 bitcast_convert_fusion
  177.0 1.9 copy.13
  178.9 11.2 %fusion.38 = f32[2048,384]{0,1:T(8,128)S(1)} fusion(bf16[2048,4096]{1,0:T(8,128)(2,1)} %get-tuple-element.10, bf16[4096,384]{1,0:T(8,128)(2,1)} %get-tuple-element.12), kind=kOutput, calls=%fused_computation.57 | convolution fusion | flops 6442450944 | bytes 23068672 | tf_op jit(solution)/shard_map/dot_general | solution.py:339
  190.1 0.1 slice.70
  190.2 1.2 fusion.9
  191.5 15.9 %fusion.2 = (f32[]{:T(128)}, bf16[4096,384]{1,0:T(8,128)(2,1)}) fusion(f32[4096]{0:T(1024)S(1)} %bitcast.22, f32[4096]{0:T(1024)S(1)} %bitcast.19, pred[384]{0:T(512)(128)(4,1)S(1)} %iota_compare_fusion, bf16[2048,4096]{1,0:T(8,128)(2,1)} %get-tuple-element.10, bf16[2048,128]{0,1:T(8,128)(2,1)S(1)} %slice.74, bf16[2048,64]{0,1:T(8,128)(2,1)S(1)} %slice.73, ...), kind=kOutput, calls=%fused_computation.5 | convolution fusion | flops 6456606720 | bytes 21528964 | tf_op jit(solution)/shard_map/dot_general | solution.py:345
  207.4 1.2 broadcast_in_dim.38.part_ref
  208.7 14.9 %total_sum.1 = f32[8,128]{1,0:T(8,128)} custom-call(f32[8,128]{1,0:T(8,128)} %broadcast_in_dim.38.part_ref), custom_call_target="tpu_custom_call" | custom-call | tf_op jit(solution)/shard_map/total_sum/pallas_call | solution.py:196
  223.5 1.2 slice.62
  225.5 12.5 %fusion.33 = f32[2048,384]{0,1:T(8,128)S(1)} fusion(bf16[2048,4096]{1,0:T(8,128)(2,1)} %get-tuple-element.10, bf16[4096,384]{1,0:T(8,128)(2,1)} %get-tuple-element.30, bf16[4096,384]{1,0:T(8,128)(2,1)} %get-tuple-element.12, f32[]{:T(128)S(6)} %div.14, f32[4096]{0:T(1024)S(1)} %bitcast.23, f32[4096]{0:T(1024)S(1)} %bitcast.20, ...), kind=kOutput, calls=%fused_computation.53 | convolution fusion | flops 6453460992 | bytes 26247556 | tf_op jit(solution)/shard_map/dot_general | solution.py:339
  238.1 0.1 slice.75
  238.2 1.2 fusion.16
  239.5 0.5 copy-done.7
  240.0 1.0 copy-done.8
  241.0 16.7 %multiply_reduce_fusion = (f32[4096]{0:T(1024)}, bf16[4096,384]{1,0:T(8,128)(2,1)}) fusion(bf16[4096,384]{1,0:T(8,128)(2,1)S(1)} %copy-done.8, f32[4096]{0:T(1024)S(1)} %bitcast.24, f32[4096]{0:T(1024)S(1)} %bitcast.21, pred[384]{0:T(512)(128)(4,1)S(1)} %iota_compare_fusion, f32[]{:T(128)S(6)} %div.14, bf16[4096,384]{1,0:T(8,128)(2,1)S(1)} %copy-done.7, ...), kind=kOutput, calls=%fused_computation.6 | convolution fusion | flops 6464466944 | bytes 27836804 | tf_op jit(solution)/shard_map/dot_general | solution.py:345
  257.7 77.8 %collect.1 = (bf16[8,512,384]{2,1,0:T(8,128)(2,1)}, f32[8,128]{1,0:T(8,128)}) custom-call(bf16[8,512,384]{2,1,0:T(8,128)(2,1)} %bitcast.17, f32[4,8,128]{2,1,0:T(8,128)} %bitcast.18), custom_call_target="tpu_custom_call" | custom-call | tf_op jit(solution)/shard_map/collect/pallas_call | solution.py:247
  335.5 1.3 bitcast_divide_fusion
  336.8 1.9 copy-done.1
  338.7 4.4 %in_place.1 = (f32[512,1536]{1,0:T(8,128)}, f32[512,1536]{1,0:T(8,128)}) custom-call(bf16[8,512,384]{2,1,0:T(8,128)(2,1)S(1)} %copy-done.1), custom_call_target="tpu_custom_call" | custom-call | tf_op jit(solution)/shard_map/in_place/pallas_call | solution.py:326
  (21 shorter events, 0.3 us)
Async XLA Ops:
  0.6 13.4 %copy-start.2 = (bf16[256,1536]{1,0:T(8,128)(2,1)S(1)}, bf16[256,1536]{1,0:T(8,128)(2,1)}, u32[]{:S(2)}) copy-start(bf16[256,1536]{1,0:T(8,128)(2,1)} %b_ref.3) | copy-start | bytes 2359300
  0.6 14.4 %copy-start.4 = (bf16[512,1536]{1,0:T(8,128)(2,1)S(1)}, bf16[512,1536]{1,0:T(8,128)(2,1)}, u32[]{:S(2)}) copy-start(bf16[512,1536]{1,0:T(8,128)(2,1)} %a_ref.2) | copy-start | bytes 4718596
  11.0 4.0 %copy-start.5 = (bf16[512,1536]{1,0:T(8,128)(2,1)S(1)}, bf16[512,1536]{1,0:T(8,128)(2,1)}, u32[]{:S(2)}) copy-start(bf16[512,1536]{1,0:T(8,128)(2,1)} %b_ref.2) | copy-start | bytes 4718596
  14.2 0.9 copy-start.3
  16.2 1.7 copy-start
  238.2 1.9 copy-start.7
  238.2 2.8 copy-start.8
  257.7 77.8 %copy-start.6 = (f32[1024]{0:T(1024)S(1)}, f32[1024]{0:T(1024)}, u32[]{:S(2)}) copy-start(f32[1024]{0:T(1024)} %param.8) | copy-start | bytes 12292
  336.8 1.9 copy-start.1
